TPU v7x, 512 devices: a whole 4x8x8 slice. The times are simulated.
512 devices in a mesh: shot: 8 (over z_lo, core), space: 64 (over y, z_hi, x).
Axes of the slice: x: 4, y: 8, z: 8 (z_hi: 2, z_lo: 4; z = z_hi * 4 + z_lo), core: 2. Of those that a mesh axis runs over, the one named last changes fastest.
Arguments:
- velocity_term: float32 [512, 64, 128], P('space'), may hold values from 0.05 to 0.2
- forward_previous: float32 [8, 512, 64, 128], P('shot', 'space'), may hold values from -6 to 6
- forward_current: float32 [8, 512, 64, 128], P('shot', 'space'), may hold values from -6 to 6
- adjoint_previous: float32 [8, 512, 64, 128], P('shot', 'space'), may hold values from -6 to 6
- adjoint_current: float32 [8, 512, 64, 128], P('shot', 'space'), may hold values from -6 to 6
- source_cell: int32 [8], P('shot'), may hold values from 0 to 4194303
- wavelet: float32 [8, 2], P('shot'), may hold values from -40 to 40
- trace_cells: int32 [8, 512, 8], P('shot'), may hold values from 0 to 4194303, as said below
- trace_weights: float32 [8, 512, 8], P('shot'), may hold values from -2 to 2
- observed: float32 [8, 2, 512], P('shot', None, 'space'), may hold values from -6 to 6
Outputs:
- forward_next: float32 [8, 512, 64, 128], P('shot', 'space')
- adjoint_next: float32 [8, 512, 64, 128], P('shot', 'space')
- residual: float32 [8, 2, 512], P('shot', None, 'space')
- gradient: float32 [512, 64, 128], P('space', 'shot')
Inputs may be any that keep to these rules, and one draw needn't show every extreme that they name: `trace_cells`: each trace's footprint is 8 cells in a row along the first dimension at one position of the other two; a trace lies in the first quarter of the first dimension with chance about one half.
All inputs are finite; a program needn't handle non-finite values.
Results may differ from a plain program's by a relative error of at most 0.0001.
Values sent between devices are 32-bit elements; how exact they have to be, the bound alone decides.
A program may use at most 64 MiB of HBM per device.

v0:
```python
import jax
import jax.numpy as jnp
from jax import lax
from jax.sharding import PartitionSpec as P

coeffs = (-205.0 / 72.0, 8.0 / 5.0, -1.0 / 5.0, 8.0 / 315.0, -1.0 / 560.0)


def padded_2(cells, sides, width):
    for axis, dim in sides:
        count = lax.axis_size(axis)
        ends = count - 1
        head = lax.slice_in_dim(cells, 0, width, axis=dim)
        tail = lax.slice_in_dim(cells, cells.shape[dim] - width, cells.shape[dim], axis=dim)
        cells = jnp.concatenate(
            [
                lax.ppermute(tail, axis, [(i, (i + 1) % count) for i in range(ends)]),
                cells,
                lax.ppermute(head, axis, [((i + 1) % count, i) for i in range(ends)]),
            ],
            axis=dim,
        )
    return cells


def laplace_ext(field):
    count = field.shape[0] - 8
    core = field[4 : 4 + count]
    width_y = core.shape[1]
    width_z = core.shape[2]
    padded = jnp.pad(core, ((0, 0), (4, 4), (4, 4)))
    result = 3.0 * coeffs[0] * core
    for j in range(1, 5):
        along_x = field[4 + j : 4 + j + count] + field[4 - j : 4 - j + count]
        along_y = (
            padded[:, 4 + j : 4 + j + width_y, 4 : 4 + width_z]
            + padded[:, 4 - j : 4 - j + width_y, 4 : 4 + width_z]
        )
        along_z = (
            padded[:, 4 : 4 + width_y, 4 + j : 4 + j + width_z]
            + padded[:, 4 : 4 + width_y, 4 - j : 4 - j + width_z]
        )
        result = result + coeffs[j] * (along_x + along_y + along_z)
    return result


def per_device(
    velocity_term,
    forward_previous,
    forward_current,
    adjoint_previous,
    adjoint_current,
    source_cell,
    wavelet,
    trace_cells,
    trace_weights,
    observed,
):
    slab_x, width_y, width_z = velocity_term.shape
    plane = width_y * width_z
    anchor = lax.axis_index("space") * slab_x
    weights = trace_weights[0]

    def add_at(field, speed, start_x, cells, amounts):
        count = field.shape[0] * plane
        local = cells - start_x * plane
        inside = (local >= 0) & (local < count)
        clipped = jnp.clip(local, 0, count - 1)
        adds = jnp.where(inside, speed.reshape(-1)[clipped] * amounts, 0.0)
        flat = field.reshape(-1).at[clipped.reshape(-1)].add(adds.reshape(-1))
        return flat.reshape(field.shape)

    def add_source(field, speed, start_x, amount):
        return add_at(field, speed, start_x, source_cell[0].reshape(1), amount.reshape(1))

    def add_inject(field, speed, start_x, values):
        return add_at(field, speed, start_x, trace_cells[0], weights * values[:, None])

    own_local = trace_cells[0] - anchor * plane
    own_inside = (own_local >= 0) & (own_local < slab_x * plane)
    own_clipped = jnp.clip(own_local, 0, slab_x * plane - 1)

    def sample(field):
        return jnp.sum(
            jnp.where(own_inside, field.reshape(-1)[own_clipped] * weights, 0.0), axis=-1
        )

    p_before = forward_previous[0]
    p_now = forward_current[0]
    a_before = adjoint_previous[0]
    a_now = adjoint_current[0]
    first = padded_2(jnp.stack([p_now, a_now]), (("space", 1),), 4)
    lap_zero = laplace_ext(first[0])
    lap_adjoint = laplace_ext(first[1])
    p_one = add_source(
        2.0 * p_now - p_before + velocity_term * lap_zero, velocity_term, anchor, wavelet[0, 0]
    )
    lap_one = laplace_ext(padded_2(p_one, (("space", 0),), 4))
    p_two = add_source(
        2.0 * p_one - p_now + velocity_term * lap_one, velocity_term, anchor, wavelet[0, 1]
    )
    partials = jnp.stack([sample(p_one), sample(p_two)])
    synthetic_own = lax.psum_scatter(partials, "space", scatter_dimension=1, tiled=True)
    misfit_own = synthetic_own - observed[0]
    misfit_all = lax.all_gather(misfit_own, "space", axis=1, tiled=True)
    a_one = add_inject(
        2.0 * a_now - a_before + velocity_term * lap_adjoint, velocity_term, anchor, misfit_all[1]
    )
    lap_adj_one = laplace_ext(padded_2(a_one, (("space", 0),), 4))
    a_two = add_inject(
        2.0 * a_one - a_now + velocity_term * lap_adj_one, velocity_term, anchor, misfit_all[0]
    )
    terms = a_one * lap_one + a_two * lap_zero
    scale = 1.0 / (lax.axis_size("shot") * forward_current.shape[0])
    gradient = lax.psum_scatter(terms, "shot", scatter_dimension=1, tiled=True) * scale
    return (p_two[None], a_two[None], misfit_own[None], gradient)


def solution(mesh):
    placed = (
        P("space", None, None),
        P("shot", "space", None, None),
        P("shot", "space", None, None),
        P("shot", "space", None, None),
        P("shot", "space", None, None),
        P("shot"),
        P("shot", None),
        P("shot", None, None),
        P("shot", None, None),
        P("shot", None, "space"),
    )
    return jax.shard_map(
        per_device,
        mesh=mesh,
        in_specs=placed,
        out_specs=(
            P("shot", "space", None, None),
            P("shot", "space", None, None),
            P("shot", None, "space"),
            P("space", "shot", None),
        ),
        check_vma=False,
    )
```

profile of v0, /device:TPU:1, one launch (start us, length us, event | category | flops | bytes accessed | tf_op | source)
XLA Modules:
  0.0 706.1 jit_solution(15188208120196253433)
XLA Ops:
  7.2 1.0 constant_dynamic-update-slice_fusion.1
  8.3 4.0 collective-permute-start.1
  12.3 1.3 collective-permute-start
  18.0 40.5 %gather_fusion = f32[4096]{0:T(1024)} fusion(f32[65536]{0:T(1024)S(1)} %bitcast.176, s32[4096]{0:T(1024)S(1)} %broadcast_clamp_fusion), kind=kCustom, calls=%fused_computation | custom fusion | bytes 49152 | tf_op jit(solution)/shard_map/gather | solution.py:69
  58.5 1.3 dynamic-slice.21
  61.1 1.3 fusion.154
  62.4 2.1 fusion.155
  64.5 23.0 %gather_fusion.1 = f32[4096]{0:T(1024)S(1)} fusion(f32[65536]{0:T(1024)S(1)} %fusion.155, s32[4096]{0:T(1024)S(1)} %broadcast_clamp_fusion), kind=kCustom, calls=%fused_computation.1 | custom fusion | bytes 49152 | tf_op jit(solution)/shard_map/gather | solution.py:85
  87.6 4.1 collective-permute-start.3
  91.7 1.3 collective-permute-start.2
  93.8 3.6 collective-permute-done.2
  98.1 2.1 fusion.156
  100.2 23.0 %gather_fusion.2 = f32[4096]{0:T(1024)S(1)} fusion(f32[65536]{0:T(1024)S(1)} %fusion.156, s32[4096]{0:T(1024)S(1)} %broadcast_clamp_fusion), kind=kCustom, calls=%fused_computation.2 | custom fusion | bytes 49152 | tf_op jit(solution)/shard_map/gather | solution.py:85
  123.5 0.8 copy-done.6
  124.6 201.4 %all-reduce.4 = f32[2,512]{1,0:T(2,128)S(1)} all-reduce(f32[2,512]{1,0:T(2,128)S(1)} %pad_maximum_fusion.6), channel_id=2, replica_groups=mesh['shot'=8,'space'=64] {'space'}, use_global_device_ids=true, to_apply=%region_2.3.clone | all-reduce | flops 1024 | bytes 8192
  326.7 185.0 %all-gather = f32[64,8,2]{1,2,0:T(2,128)S(1)} all-gather(f32[1,8,2]{1,2,0:T(2,128)S(1)} %get-tuple-element.57), channel_id=1, replica_groups=mesh['shot'=8,'space'=64] {'space'}, dimensions={0}, use_global_device_ids=true | all-gather | bytes 4160 | tf_op jit(solution)/shard_map/all_gather | solution.py:105
  513.0 28.6 %scatter_fusion = f32[65536]{0:T(1024)S(1)} fusion(f32[65536]{0:T(1024)S(1)} %bitcast.183, s32[4096]{0:T(1024)S(1)} %bitcast.191, f32[4096]{0:T(1024)S(1)} %get-tuple-element.55), kind=kCustom, calls=%fused_computation.3 | custom fusion | flops 4096 | bytes 65536 | tf_op jit(solution)/shard_map/scatter-add | solution.py:70
  541.7 2.8 collective-permute-start.5
  544.5 1.3 collective-permute-start.4
  546.4 3.8 collective-permute-done.4
  550.9 28.6 %scatter_fusion.1 = f32[65536]{0:T(1024)S(1)} fusion(f32[65536]{0:T(1024)S(1)} %bitcast.186, s32[4096]{0:T(1024)S(1)} %bitcast.192, f32[4096]{0:T(1024)S(1)} %get-tuple-element.54), kind=kCustom, calls=%fused_computation.4 | custom fusion | flops 4096 | bytes 65536 | tf_op jit(solution)/shard_map/scatter-add | solution.py:70
  579.5 0.8 multiply_add_fusion
  580.3 117.6 %reduce-scatter.3.cloned.1.call-done = f32[8,8,128]{2,1,0:T(8,128)} async-done(((f32[8,64,128]{2,1,0:T(8,128)}), f32[8,8,128]{2,1,0:T(8,128)}) %reduce-scatter.3.cloned.1.call-update) | async-done | bytes 32784 | tf_op jit(solution)/shard_map/reduce_scatter | solution.py:115
  697.9 1.4 broadcast_multiply_fusion
  (75 shorter events, 9.2 us)
Async XLA Ops:
  7.2 1.1 copy-start.7
  7.2 690.7 %reduce-scatter.3.cloned.1.call-start = ((), (), s32[]{:S(2)}) async-start(), calls=%async_computation.1 | async-start | bytes 294912 | tf_op jit(solution)/shard_map/reduce_scatter | solution.py:115
  8.3 5.9 copy-start.16
  8.3 52.8 %collective-permute-start.1 = (f32[2,4,64,128]{3,2,1,0:T(8,128)S(1)}, f32[2,4,64,128]{3,2,1,0:T(8,128)S(1)}, u32[]{:S(2)}, u32[]{:S(2)}) collective-permute-start(f32[2,4,64,128]{3,2,1,0:T(8,128)S(1)} %get-tuple-element.49), channel_id=1, source_target_pairs={{0,1},{1,2},{2,3},{3,4},{4,5},{5,6},{6,7},{7,8},{8,9},{9,10},{10,1... | collective-permute-start | bytes 786440 | tf_op jit(solution)/shard_map/ppermute | solution.py:17
  12.3 48.8 %collective-permute-start = (f32[2,4,64,128]{3,2,1,0:T(8,128)S(1)}, f32[2,4,64,128]{3,2,1,0:T(8,128)S(1)}, u32[]{:S(2)}, u32[]{:S(2)}) collective-permute-start(f32[2,4,64,128]{3,2,1,0:T(8,128)S(1)} %get-tuple-element.48), channel_id=1, source_target_pairs={{1,0},{2,1},{3,2},{4,3},{5,4},{6,5},{7,6},{8,7},{9,8},{10,9},{11,1... | collective-permute-start | bytes 786440 | tf_op jit(solution)/shard_map/ppermute | solution.py:19
  16.6 1.4 copy-start
  16.7 41.8 %copy-start.5 = (f32[1,512,8]{2,1,0:T(8,128)}, f32[1,512,8]{2,1,0:T(8,128)S(1)}, u32[]{:S(2)}) copy-start(f32[1,512,8]{2,1,0:T(8,128)S(1)} %copy.19) | copy-start | bytes 49156
  18.0 43.1 %copy-start.4 = (f32[1,8,64,128]{3,2,1,0:T(8,128)S(1)}, f32[1,8,64,128]{3,2,1,0:T(8,128)}, u32[]{:S(2)}) copy-start(f32[1,8,64,128]{3,2,1,0:T(8,128)} %param.16) | copy-start | bytes 786436
  18.0 43.1 %copy-start.12 = (f32[1,8,64,128]{3,2,1,0:T(8,128)S(1)}, f32[1,8,64,128]{3,2,1,0:T(8,128)}, u32[]{:S(2)}) copy-start(f32[1,8,64,128]{3,2,1,0:T(8,128)} %param.15) | copy-start | bytes 786436
  64.5 28.7 %copy-start.13 = (f32[1,8,64,128]{3,2,1,0:T(8,128)S(1)}, f32[1,8,64,128]{3,2,1,0:T(8,128)}, u32[]{:S(2)}) copy-start(f32[1,8,64,128]{3,2,1,0:T(8,128)} %param.17) | copy-start | bytes 786436
  87.6 5.6 copy-start.8
  87.6 6.2 collective-permute-start.3
  91.7 5.7 collective-permute-start.2
  100.2 23.0 %copy-start.1 = (f32[65536]{0:T(1024)}, f32[65536]{0:T(1024)S(1)}, u32[]{:S(2)}) copy-start(f32[65536]{0:T(1024)S(1)} %fusion.156) | copy-start | bytes 786436
  100.2 23.2 %copy-start.10 = (s32[1,512,8]{2,1,0:T(8,128)S(1)}, s32[1,512,8]{2,1,0:T(8,128)}, u32[]{:S(2)}) copy-start(s32[1,512,8]{2,1,0:T(8,128)} %copy-done.9) | copy-start | bytes 49156
  123.3 1.0 copy-start.6
  123.3 389.7 %copy-start.14 = (s32[4096,1]{0,1:T(1,128)S(1)}, s32[4096,1]{0,1:T(1,128)}, u32[]{:S(2)}) copy-start(s32[4096,1]{0,1:T(1,128)} %compare_select_fusion.1) | copy-start | bytes 49156
  124.6 201.4 %copy-start.19 = (f32[1,2,8]{2,1,0:T(2,128)S(1)}, f32[1,2,8]{2,1,0:T(2,128)}, u32[]{:S(2)}) copy-start(f32[1,2,8]{2,1,0:T(2,128)} %param.23) | copy-start | bytes 196
  512.2 0.7 copy-start.3
  512.3 0.7 copy-start.15
  541.7 4.8 collective-permute-start.5
  544.5 5.7 collective-permute-start.4
  550.8 28.7 %copy-start.11 = (f32[8,64,128]{2,1,0:T(8,128)S(1)}, f32[8,64,128]{2,1,0:T(8,128)}, u32[]{:S(2)}) copy-start(f32[8,64,128]{2,1,0:T(8,128)} %get-tuple-element.47) | copy-start | bytes 786436
  579.5 0.8 copy-start.2
  (3 other events, 2.1 us)
Sparse Core Ops, SparseCore 0:
  580.4 117.4 reduce-scatter.2
where the time goes:
time: 709 us; the launch traced here: 706 us
  blocking collectives  386 us (54%)
  waiting for transfers between devices  126 us (18%)
  local copies, waits for them, and re-layouts  94.6 us (13%)
  other arithmetic  68.4 us (10%)
  between operations  16.2 us (2%)
  starting transfers between devices  14.8 us (2%)
    unnamed x1, blocking collectives  201 us
    all_gather x1, blocking collectives, per_device(): misfit_all = lax.all_gather(misfit_own, 'space', axis=1, tiled=True)  185 us
    reduce_scatter x1, waiting for transfers between devices, per_device(): lax.psum_scatter(terms, 'shot', scatter_dimension=1, tiled=True) * scale  118 us
    scatter-add x4, other arithmetic, add_at(): flat = field.reshape(-1).at[clipped.reshape(-1)].add(adds.reshape(-1))  61.5 us
    gather x4, local copies, waits for them, and re-layouts, sample(): field.reshape(-1)[own_clipped] * weights  46.4 us
    gather x1, local copies, waits for them, and re-layouts, add_at(): adds = jnp.where(inside, speed.reshape(-1)[clipped] * amounts, 0.0)  40.5 us
  transfers between devices with their start and end apart: 7, of which 4 were waited for; matrix products, arithmetic and copies ran while one was open for 6% of the time, Pallas kernels for 0%

commit v1 on v0

v1 whole, which is shorter than its diff:
```python
import functools

import jax
import jax.numpy as jnp
from jax import lax
from jax.experimental import pallas as pl
from jax.experimental.pallas import tpu as pltpu
from jax.sharding import PartitionSpec as P

MESH = pl.DeviceIdType.MESH
F32, BF16 = jnp.float32, jnp.bfloat16
coeffs = (-205.0 / 72.0, 8.0 / 5.0, -1.0 / 5.0, 8.0 / 315.0, -1.0 / 560.0)
whole = (8064.0, -1008.0, 128.0, -9.0)


def split(f):
    hi = f.astype(BF16)
    return hi, (f - hi.astype(F32)).astype(BF16)


def dot(a, b):
    return jnp.dot(a, b, preferred_element_type=F32)


def band(i, j):
    d = jnp.abs(i - j)
    m = jnp.zeros(d.shape, F32)
    for k, c in enumerate(whole):
        m = jnp.where(d == k + 1, c, m)
    return m.astype(BF16)


def iota(shape, dim):
    return lax.broadcasted_iota(jnp.int32, shape, dim)


def lap_inside(f, dz, dy):
    rows, ny, nz = f.shape
    hi, lo = split(f)
    zz = dot(jnp.concatenate([hi.reshape(rows * ny, nz), lo.reshape(rows * ny, nz)], axis=1), dz)
    yy = dot(dy, jnp.concatenate([jnp.concatenate([hi[x], lo[x]], axis=0) for x in range(rows)], axis=1))
    out = []
    for x in range(rows):
        r = 3.0 * coeffs[0] * f[x] + (zz[x * ny : (x + 1) * ny] + yy[:, x * nz : (x + 1) * nz]) * (1.0 / 5040.0)
        for j in range(1, 5):
            terms = [f[k] for k in (x - j, x + j) if 0 <= k < rows]
            if terms:
                r = r + coeffs[j] * functools.reduce(jnp.add, terms)
        out.append(r)
    return out


def from_left(h, i, edge):
    return functools.reduce(jnp.add, [(coeffs[j] * edge) * h[4 + i - j] for j in range(i + 1, 5)])


def from_right(h, i, edge):
    return functools.reduce(jnp.add, [(coeffs[j] * edge) * h[i + j - 4] for j in range(4 - i, 5)])


def kernel(
    sizes,
    v_in, pm_in, p0_in, am_in, a0_in, cell_in, wave_in, cells_in, weights_in, obs_in,
    f_out, a_out, r_out, g_out,
    V, PM, P0, AM, A0, LAP0, P1, LAP1, P2, A1, A2, INJ0, terms, grad,
    cell, wave, cells, weights, obs, obs_wide, res,
    halo, ozT, oz, oyT, wx, dz, dy,
    part, part_in, arow, sums, sums_y, sums_z, sums_x, gin,
    load_sem, out_sem, send_sem, recv_sem,
):
    n_shot, n_space, nx_, nz_, ny_ = sizes
    rows, ny, nz = V.shape
    traces = weights.shape[1]
    blocks = traces // 128
    h = lax.axis_index("shot")
    s = lax.axis_index("space")
    x, zh, y = s % nx_, (s // nx_) % nz_, s // (nx_ * nz_)

    def ring(k):
        return (h, (s + k + n_space) % n_space)

    def slab(x, zh, y):
        return (h, (y * nz_ + zh) * nx_ + x)

    to_y = [slab(x, zh, (y + k) % ny_) for k in range(1, ny_)]
    to_z = [slab(x, (zh + k) % nz_, y) for k in range(1, nz_)]
    to_x = [slab((x + k) % nx_, zh, y) for k in range(1, nx_)]
    to_shot = [((h + k) % n_shot, s) for k in range(1, n_shot)]
    near = [ring(1), ring(-1), ring(2), ring(-2)]

    barrier = pltpu.get_barrier_semaphore()
    partners = near + to_z + to_y + to_x + to_shot
    for d in partners:
        pl.semaphore_signal(barrier, inc=1, device_id=d, device_id_type=MESH)

    loads = [
        pltpu.make_async_copy(a, b, load_sem.at[i])
        for i, (a, b) in enumerate(
            (
                (cells_in, cells), (weights_in, weights), (p0_in, P0), (v_in, V), (pm_in, PM),
                (cell_in, cell), (wave_in, wave), (a0_in, A0), (am_in, AM), (obs_in, obs),
            )
        )
    ]
    for c in loads:
        c.start()

    sent = []

    def send(src, dst, to):
        i = len(sent)
        c = pltpu.make_async_remote_copy(
            src_ref=src, dst_ref=dst, send_sem=send_sem.at[i], recv_sem=recv_sem.at[i], device_id=to, device_id_type=MESH
        )
        c.start()
        sent.append(c)
        return c

    lo4, hi4 = pl.ds(0, 4), pl.ds(rows - 4, 4)

    dz[...] = band(iota((2 * nz, nz), 0) % nz, iota((2 * nz, nz), 1))
    dy[...] = band(iota((ny, 2 * ny), 0), iota((ny, 2 * ny), 1) % ny)

    loads[0].wait()
    loads[1].wait()
    at = cells[...]
    at_z = at[0:1] & (nz - 1)
    at_y = (at[0:1] // nz) & (ny - 1)
    hot = jnp.where(iota((nz, traces), 0) == at_z, 1.0, 0.0)
    ozT[pl.ds(0, nz)] = hot.astype(BF16)
    ozT[pl.ds(nz, nz)] = hot.astype(BF16)
    hot_t = jnp.transpose(hot).astype(BF16)
    oz[pl.ds(0, traces)] = hot_t
    oz[pl.ds(traces, traces)] = hot_t
    oyT[...] = jnp.where(iota((ny, traces), 0) == at_y, 1.0, 0.0).astype(BF16)
    at_x = at // (nz * ny) - s * rows + 4
    w = weights[...]
    acc = jnp.zeros((rows + 8, traces), F32)
    row_id = iota((rows + 8, traces), 0)
    for k in range(at.shape[0]):
        acc = acc + jnp.where(at_x[k : k + 1] == row_id, w[k : k + 1], 0.0)
    wx[...] = acc

    left_edge = jnp.where(s > 0, 1.0, 0.0).astype(F32)
    right_edge = jnp.where(s < n_space - 1, 1.0, 0.0).astype(F32)

    for k in (2, 3, 4, 5, 6):
        loads[k].wait()
    place = cell[...] - s * (rows * ny * nz)
    flat = iota((ny, nz), 0) * nz + iota((ny, nz), 1)
    spots = [jnp.where(flat + i * (ny * nz) == place, 1.0, 0.0) for i in range(rows)]
    p0 = P0[...]
    lap = lap_inside(p0, dz[...], dy[...])
    for i in range(rows):
        LAP0[i] = lap[i]
        P1[i] = 2.0 * p0[i] - PM[i] + V[i] * (lap[i] + spots[i] * wave[0:1, 0:1])
    loads[7].wait()
    loads[8].wait()
    a0 = A0[...]
    lap = lap_inside(a0, dz[...], dy[...])
    for i in range(rows):
        A1[4 + i] = 2.0 * a0[i] - AM[i] + V[i] * lap[i]

    loads[9].wait()
    lane0, row0 = (s * 8) % 128, (s * 8) // 128
    obs_wide[...] = jnp.zeros(obs_wide.shape, F32)
    obs_wide[pl.ds(0, 2), pl.ds(0, 8)] = obs[...]
    rolled = pltpu.roll(obs_wide[...], lane0, 1)
    which = iota((8, 128), 0)
    sums[0] = jnp.where(which == row0, rolled[0:1], 0.0) + jnp.where(which == blocks + row0, rolled[1:2], 0.0)

    pl.semaphore_wait(barrier, len(partners))

    def exchange(field, low, high):
        a = send(low, halo.at[field, 1], ring(-1))
        b = send(high, halo.at[field, 0], ring(1))
        return b, a

    got_p0 = exchange(0, p0_in.at[lo4], p0_in.at[hi4])
    got_a0 = exchange(1, a0_in.at[lo4], a0_in.at[hi4])
    obs_y = [send(sums.at[0], sums_y.at[0, k], d) for k, d in enumerate(to_y)]
    got_v = exchange(2, v_in.at[lo4], v_in.at[hi4])

    got_p0[0].wait_recv()
    hl = halo[0, 0]
    for i in range(4):
        add = from_left(hl, i, left_edge)
        LAP0[i] += add
        P1[i] += V[i] * add
    p1_left = send(P1.at[lo4], halo.at[3, 1], ring(-1))
    got_p0[1].wait_recv()
    hr = halo[0, 1]
    for i in range(4):
        add = from_right(hr, i, right_edge)
        LAP0[rows - 4 + i] += add
        P1[rows - 4 + i] += V[rows - 4 + i] * add
    p1_right = send(P1.at[hi4], halo.at[3, 0], ring(1))

    def sample(f, k):
        hi, lo = split(f)
        g = dot(jnp.concatenate([hi.reshape(rows * ny, nz), lo.reshape(rows * ny, nz)], axis=1), ozT[...])
        acc = wx[4:5] * g[0:ny]
        for i in range(1, rows):
            acc = acc + wx[4 + i : 5 + i] * g[i * ny : (i + 1) * ny]
        line = jnp.sum(acc * oyT[...].astype(F32), axis=0, keepdims=True)
        part[k] = jnp.zeros((8, 128), F32)
        for b in range(blocks):
            part[k, pl.ds(k * blocks + b, 1), :] = line[:, b * 128 : (b + 1) * 128]
        return [send(part.at[k], part_in.at[k, i], d) for i, d in enumerate(near)]

    p1 = P1[...]
    got_part = [sample(p1, 0)]
    lap = lap_inside(p1, dz[...], dy[...])
    for i in range(rows):
        LAP1[i] = lap[i]
        P2[i] = 2.0 * p1[i] - P0[i] + V[i] * (lap[i] + spots[i] * wave[0:1, 1:2])

    got_a0[0].wait_recv()
    hl = halo[1, 0]
    for i in range(4):
        A1[4 + i] += V[i] * from_left(hl, i, left_edge)
    b1_left = send(A1.at[pl.ds(4, 4)], halo.at[4, 1], ring(-1))
    got_a0[1].wait_recv()
    hr = halo[1, 1]
    for i in range(4):
        A1[rows + i] += V[rows - 4 + i] * from_right(hr, i, right_edge)
    b1_right = send(A1.at[pl.ds(rows, 4)], halo.at[4, 0], ring(1))

    def gather(got, own, ref, slot, count):
        total = own
        for c in got:
            c.wait_recv()
        for k in range(count):
            total = total + ref[slot, k]
        return total

    sums[1] = gather(obs_y, sums[0], sums_y, 0, ny_ - 1)
    obs_z = [send(sums.at[1], sums_z.at[0, k], d) for k, d in enumerate(to_z)]

    p1_right.wait_recv()
    hl = halo[3, 0]
    for i in range(4):
        add = from_left(hl, i, left_edge)
        LAP1[i] += add
        P2[i] += V[i] * add
    p1_left.wait_recv()
    hr = halo[3, 1]
    for i in range(4):
        add = from_right(hr, i, right_edge)
        LAP1[rows - 4 + i] += add
        P2[rows - 4 + i] += V[rows - 4 + i] * add
    got_part.append(sample(P2[...], 1))
    outs = [pltpu.make_async_copy(P2, f_out, out_sem.at[0])]
    outs[0].start()
    sums[3] = part[0] + part[1]
    res_y = [send(sums.at[3], sums_y.at[1, k], d) for k, d in enumerate(to_y)]

    sums[2] = gather(obs_z, sums[1], sums_z, 0, nz_ - 1)
    obs_x = [send(sums.at[2], sums_x.at[0, k], d) for k, d in enumerate(to_x)]

    def inject(k, first, count):
        arow[k] = gather(got_part[k], part[k], part_in, k, 4) - observed
        line = jnp.concatenate([arow[k, pl.ds(k * blocks + b, 1), :] for b in range(blocks)], axis=1)
        hi, lo = split(wx[pl.ds(first, count)] * line)
        hot = oyT[...]
        lhs = jnp.concatenate(
            [jnp.concatenate([hot * hi[i : i + 1], hot * lo[i : i + 1]], axis=1) for i in range(count)], axis=0
        )
        return dot(lhs, oz[...])

    observed = gather(obs_x, sums[2], sums_x, 0, nx_ - 1)

    inj = inject(0, 4, rows)
    for i in range(rows):
        INJ0[i] = V[i] * inj[i * ny : (i + 1) * ny]
    got_v[0].wait_recv()
    got_v[1].wait_recv()
    b1_right.wait_recv()
    b1_left.wait_recv()
    b1_left.wait_send()
    b1_right.wait_send()
    inj = inject(1, 0, rows + 8)
    for i in range(4):
        A1[i] = halo[4, 0, i] * left_edge + halo[2, 0, i] * inj[i * ny : (i + 1) * ny]
        k = rows + 4 + i
        A1[k] = halo[4, 1, i] * right_edge + halo[2, 1, i] * inj[k * ny : (k + 1) * ny]
    for i in range(rows):
        k = 4 + i
        A1[k] += V[i] * inj[k * ny : (k + 1) * ny]
    a1 = A1[...]
    lap = lap_inside(a1[4 : 4 + rows], dz[...], dy[...])
    scale = 1.0 / n_shot
    for i in range(rows):
        lp = lap[i]
        if i < 4:
            lp = lp + from_left(a1[0:4], i, 1.0)
        if i >= rows - 4:
            lp = lp + from_right(a1[rows + 4 :], i - rows + 4, 1.0)
        a2 = 2.0 * a1[4 + i] - A0[i] + V[i] * lp + INJ0[i]
        A2[i] = a2
        terms[i] = (a1[4 + i] * LAP1[i] + a2 * LAP0[i]) * scale
    got_g = [
        send(terms.at[:, pl.ds(pl.multiple_of(d[0] * 8, 8), 8)], gin.at[k], d) for k, d in enumerate(to_shot)
    ]
    outs.append(pltpu.make_async_copy(A2, a_out, out_sem.at[1]))
    outs[1].start()

    sums[4] = gather(res_y, sums[3], sums_y, 1, ny_ - 1)
    res_z = [send(sums.at[4], sums_z.at[1, k], d) for k, d in enumerate(to_z)]
    sums[5] = gather(res_z, sums[4], sums_z, 1, nz_ - 1)
    res_x = [send(sums.at[5], sums_x.at[1, k], d) for k, d in enumerate(to_x)]

    total = terms[:, pl.ds(pl.multiple_of(h * 8, 8), 8)]
    for c in got_g:
        c.wait_recv()
    for k in range(n_shot - 1):
        total = total + gin[k]
    grad[...] = total
    outs.append(pltpu.make_async_copy(grad, g_out, out_sem.at[2]))
    outs[2].start()

    every = gather(res_x, sums[5], sums_x, 1, nx_ - 1)
    picked = jnp.concatenate(
        [
            jnp.sum(jnp.where(which == k * blocks + row0, every, 0.0), axis=0, keepdims=True)
            for k in range(2)
        ],
        axis=0,
    )
    obs_wide[pl.ds(0, 2)] = picked
    rolled = pltpu.roll(obs_wide[...], (128 - lane0) % 128, 1)
    res[...] = rolled[0:2, 0:8] - obs[...]
    outs.append(pltpu.make_async_copy(res, r_out, out_sem.at[3]))
    outs[3].start()

    for c in sent:
        if c is not b1_left and c is not b1_right:
            c.wait_send()
    for c in outs:
        c.wait()


def solution(mesh):
    n_shot, n_space = mesh.shape["shot"], mesh.shape["space"]
    sizes = (n_shot, n_space, 4, 2, n_space // 8)

    def per_device(v, pm, p0, am, a0, cell, wave, cells, weights, obs):
        rows, ny, nz = v.shape
        traces = weights.shape[1]
        slab = (rows, ny, nz)
        anywhere = pl.BlockSpec(memory_space=pl.ANY)
        vm = lambda *shape: pltpu.VMEM(shape, F32)
        count = 5 * 2 + 2 * 4 + 2 * (sizes[2] + sizes[3] + sizes[4] - 3) + n_shot - 1
        f, a, r, g = pl.pallas_call(
            functools.partial(kernel, sizes),
            out_shape=(
                jax.ShapeDtypeStruct(slab, F32),
                jax.ShapeDtypeStruct(slab, F32),
                jax.ShapeDtypeStruct((2, 8), F32),
                jax.ShapeDtypeStruct((rows, ny // n_shot, nz), F32),
            ),
            in_specs=[anywhere] * 10,
            out_specs=[anywhere] * 4,
            scratch_shapes=[vm(*slab)] * 9
            + [vm(rows + 8, ny, nz), vm(*slab), vm(*slab), vm(*slab), vm(rows, ny // n_shot, nz)]
            + [
                pltpu.VMEM((1, 1), jnp.int32),
                vm(1, 2),
                pltpu.VMEM((8, traces), jnp.int32),
                vm(8, traces),
                vm(2, 8),
                vm(8, 128),
                vm(2, 8),
                vm(5, 2, 4, ny, nz),
                pltpu.VMEM((2 * nz, traces), BF16),
                pltpu.VMEM((2 * traces, nz), BF16),
                pltpu.VMEM((ny, traces), BF16),
                vm(rows + 8, traces),
                pltpu.VMEM((2 * nz, nz), BF16),
                pltpu.VMEM((ny, 2 * ny), BF16),
                vm(2, 8, 128),
                vm(2, 4, 8, 128),
                vm(2, 8, 128),
                vm(6, 8, 128),
                vm(2, sizes[4] - 1, 8, 128),
                vm(2, sizes[3] - 1, 8, 128),
                vm(2, sizes[2] - 1, 8, 128),
                vm(n_shot - 1, rows, ny // n_shot, nz),
                pltpu.SemaphoreType.DMA((10,)),
                pltpu.SemaphoreType.DMA((4,)),
                pltpu.SemaphoreType.DMA((count,)),
                pltpu.SemaphoreType.DMA((count,)),
            ],
            compiler_params=pltpu.CompilerParams(collective_id=0, has_side_effects=True, vmem_limit_bytes=40 << 20),
            cost_estimate=pl.CostEstimate(flops=10**9, bytes_accessed=2 << 20, transcendentals=0),
            name="two_steps",
        )(
            v, pm[0], p0[0], am[0], a0[0], cell.reshape(1, 1), wave,
            jnp.transpose(cells[0]), jnp.transpose(weights[0]), obs[0],
        )
        return f[None], a[None], r[None], g

    field = P("shot", "space", None, None)
    return jax.shard_map(
        per_device,
        mesh=mesh,
        in_specs=(
            P("space", None, None), field, field, field, field,
            P("shot"), P("shot", None), P("shot", None, None), P("shot", None, None), P("shot", None, "space"),
        ),
        out_specs=(field, field, P("shot", None, "space"), P("space", "shot", None)),
        check_vma=False,
    )
```

time: 709 us -> 74.7 us (0.11)
  the two profiles are of different devices: /device:TPU:1 before, /device:TPU:64 now
where the time goes in v1:
time: 74.7 us; the launch traced here: 74.3 us
  Pallas kernels  63.6 us (85%)
  local copies, waits for them, and re-layouts  9.38 us (13%)
  between operations  1.33 us (2%)
    pallas_call x1, Pallas kernels, per_device(): pl.pallas_call(functools.partial(kernel, sizes), out_shape=(jax.ShapeDtyp...  63.6 us
    unnamed x22, local copies, waits for them, and re-layouts  9.38 us

profile of v1, /device:TPU:64, one launch (start us, length us, event | category | flops | bytes accessed | tf_op | source)
XLA Modules:
  0.0 74.3 jit_solution(9159788426156390977)
XLA Ops:
  0.6 0.0 copy-start.5
  1.3 0.0 copy-start.7
  1.3 0.0 copy-done.5
  1.4 0.6 copy-done.7
  2.0 0.0 copy-start
  2.0 0.9 %copy-done = f32[8,64,128]{2,1,0:T(8,128)S(1)} copy-done((f32[8,64,128]{2,1,0:T(8,128)S(1)}, f32[8,64,128]{2,1,0:T(8,128)}, u32[]{:S(2)}) %copy-start) | copy-done | bytes 262168
  2.9 0.0 copy-start.1
  2.9 0.9 %copy-done.1 = f32[1,8,64,128]{3,2,1,0:T(8,128)S(1)} copy-done((f32[1,8,64,128]{3,2,1,0:T(8,128)S(1)}, f32[1,8,64,128]{3,2,1,0:T(8,128)}, u32[]{:S(2)}) %copy-start.1) | copy-done | bytes 262168
  3.9 0.0 copy-start.2
  3.9 0.9 %copy-done.2 = f32[1,8,64,128]{3,2,1,0:T(8,128)S(1)} copy-done((f32[1,8,64,128]{3,2,1,0:T(8,128)S(1)}, f32[1,8,64,128]{3,2,1,0:T(8,128)}, u32[]{:S(2)}) %copy-start.2) | copy-done | bytes 262168
  4.8 0.0 copy-start.3
  4.8 0.9 %copy-done.3 = f32[1,8,64,128]{3,2,1,0:T(8,128)S(1)} copy-done((f32[1,8,64,128]{3,2,1,0:T(8,128)S(1)}, f32[1,8,64,128]{3,2,1,0:T(8,128)}, u32[]{:S(2)}) %copy-start.3) | copy-done | bytes 262168
  5.8 0.0 copy-start.4
  5.8 0.9 %copy-done.4 = f32[1,8,64,128]{3,2,1,0:T(8,128)S(1)} copy-done((f32[1,8,64,128]{3,2,1,0:T(8,128)S(1)}, f32[1,8,64,128]{3,2,1,0:T(8,128)}, u32[]{:S(2)}) %copy-start.4) | copy-done | bytes 262168
  6.7 0.0 copy-start.6
  6.7 0.7 copy-done.6
  7.5 0.0 copy-start.8
  7.5 0.7 copy-done.8
  8.1 63.6 %two_steps.1 = (f32[8,64,128]{2,1,0:T(8,128)S(1)}, f32[8,64,128]{2,1,0:T(8,128)S(1)}, f32[2,8]{1,0:T(2,128)S(1)}, f32[8,8,128]{2,1,0:T(8,128)S(1)}) custom-call(f32[8,64,128]{2,1,0:T(8,128)S(1)} %copy-done, f32[8,64,128]{2,1,0:T(8,128)S(1)} %bitcast.19, f32[8,64,128]{2,1,0:T(8,128)S(1)} %bitcast.20, f32[8,64,128]{2,1,0:T(8,128)S(1)} %bitcast.21, ...), custom_call_target="tpu_custom_call" | custom-call | flops 1000000000 | bytes 2097152 | tf_op jit(solution)/shard_map/two_steps/pallas_call | solution.py:354
  71.7 0.7 copy.19
  72.4 0.7 copy.20
  73.1 0.6 copy.21
  73.7 0.6 copy.22
Async XLA Ops:
  0.6 0.7 copy-start.5
  1.3 0.7 copy-start.7
  2.0 0.9 %copy-start = (f32[8,64,128]{2,1,0:T(8,128)S(1)}, f32[8,64,128]{2,1,0:T(8,128)}, u32[]{:S(2)}) copy-start(f32[8,64,128]{2,1,0:T(8,128)} %v_in.1) | copy-start | bytes 786436
  2.9 0.9 %copy-start.1 = (f32[1,8,64,128]{3,2,1,0:T(8,128)S(1)}, f32[1,8,64,128]{3,2,1,0:T(8,128)}, u32[]{:S(2)}) copy-start(f32[1,8,64,128]{3,2,1,0:T(8,128)} %param.11) | copy-start | bytes 786436
  3.9 0.9 %copy-start.2 = (f32[1,8,64,128]{3,2,1,0:T(8,128)S(1)}, f32[1,8,64,128]{3,2,1,0:T(8,128)}, u32[]{:S(2)}) copy-start(f32[1,8,64,128]{3,2,1,0:T(8,128)} %param.12) | copy-start | bytes 786436
  4.8 0.9 %copy-start.3 = (f32[1,8,64,128]{3,2,1,0:T(8,128)S(1)}, f32[1,8,64,128]{3,2,1,0:T(8,128)}, u32[]{:S(2)}) copy-start(f32[1,8,64,128]{3,2,1,0:T(8,128)} %param.13) | copy-start | bytes 786436
  5.8 0.9 %copy-start.4 = (f32[1,8,64,128]{3,2,1,0:T(8,128)S(1)}, f32[1,8,64,128]{3,2,1,0:T(8,128)}, u32[]{:S(2)}) copy-start(f32[1,8,64,128]{3,2,1,0:T(8,128)} %param.14) | copy-start | bytes 786436
  6.7 0.7 copy-start.6
  7.5 0.7 copy-start.8

commit v2 on v1

--- a/solution.py
+++ b/solution.py
@@ -62,8 +62,8 @@
     sizes,
     v_in, pm_in, p0_in, am_in, a0_in, cell_in, wave_in, cells_in, weights_in, obs_in,
     f_out, a_out, r_out, g_out,
-    V, PM, P0, AM, A0, LAP0, P1, LAP1, P2, A1, A2, INJ0, terms, grad,
-    cell, wave, cells, weights, obs, obs_wide, res,
+    V, PM, P0, AM, A0, LAP0, P1, LAP1, A1, INJ0, terms, P2, A2, res, grad,
+    cell, wave, cells, weights, obs, obs_wide,
     halo, ozT, oz, oyT, wx, dz, dy,
     part, part_in, arow, sums, sums_y, sums_z, sums_x, gin,
     load_sem, out_sem, send_sem, recv_sem,
@@ -279,6 +279,8 @@
     b1_left.wait_recv()
     b1_left.wait_send()
     b1_right.wait_send()
+    sums[4] = gather(res_y, sums[3], sums_y, 1, ny_ - 1)
+    res_z = [send(sums.at[4], sums_z.at[1, k], d) for k, d in enumerate(to_z)]
     inj = inject(1, 0, rows + 8)
     for i in range(4):
         A1[i] = halo[4, 0, i] * left_edge + halo[2, 0, i] * inj[i * ny : (i + 1) * ny]
@@ -302,14 +304,12 @@
     got_g = [
         send(terms.at[:, pl.ds(pl.multiple_of(d[0] * 8, 8), 8)], gin.at[k], d) for k, d in enumerate(to_shot)
     ]
+
+    sums[5] = gather(res_z, sums[4], sums_z, 1, nz_ - 1)
+    res_x = [send(sums.at[5], sums_x.at[1, k], d) for k, d in enumerate(to_x)]
+
     outs.append(pltpu.make_async_copy(A2, a_out, out_sem.at[1]))
     outs[1].start()
-
-    sums[4] = gather(res_y, sums[3], sums_y, 1, ny_ - 1)
-    res_z = [send(sums.at[4], sums_z.at[1, k], d) for k, d in enumerate(to_z)]
-    sums[5] = gather(res_z, sums[4], sums_z, 1, nz_ - 1)
-    res_x = [send(sums.at[5], sums_x.at[1, k], d) for k, d in enumerate(to_x)]
-
     total = terms[:, pl.ds(pl.multiple_of(h * 8, 8), 8)]
     for c in got_g:
         c.wait_recv()
@@ -340,6 +340,19 @@
         c.wait()
 
 
+def store(*refs):
+    given, given_back, held, sems = refs[:4], refs[4:8], refs[8:12], refs[12]
+    loads = [pltpu.make_async_copy(a, b, sems.at[0, i]) for i, (a, b) in enumerate(zip(given, held))]
+    stores = [pltpu.make_async_copy(a, b, sems.at[1, i]) for i, (a, b) in enumerate(zip(held, given_back))]
+    for c in loads:
+        c.start()
+    for c, d in zip(loads, stores):
+        c.wait()
+        d.start()
+    for c in stores:
+        c.wait()
+
+
 def solution(mesh):
     n_shot, n_space = mesh.shape["shot"], mesh.shape["space"]
     sizes = (n_shot, n_space, 4, 2, n_space // 8)
@@ -348,21 +361,22 @@
         rows, ny, nz = v.shape
         traces = weights.shape[1]
         slab = (rows, ny, nz)
-        anywhere = pl.BlockSpec(memory_space=pl.ANY)
+        hbm = pl.BlockSpec(memory_space=pltpu.HBM)
         vm = lambda *shape: pltpu.VMEM(shape, F32)
         count = 5 * 2 + 2 * 4 + 2 * (sizes[2] + sizes[3] + sizes[4] - 3) + n_shot - 1
-        f, a, r, g = pl.pallas_call(
-            functools.partial(kernel, sizes),
-            out_shape=(
+        results = (
                 jax.ShapeDtypeStruct(slab, F32),
                 jax.ShapeDtypeStruct(slab, F32),
                 jax.ShapeDtypeStruct((2, 8), F32),
                 jax.ShapeDtypeStruct((rows, ny // n_shot, nz), F32),
-            ),
-            in_specs=[anywhere] * 10,
-            out_specs=[anywhere] * 4,
-            scratch_shapes=[vm(*slab)] * 9
-            + [vm(rows + 8, ny, nz), vm(*slab), vm(*slab), vm(*slab), vm(rows, ny // n_shot, nz)]
+            )
+        out = pl.pallas_call(
+            functools.partial(kernel, sizes),
+            out_shape=results,
+            in_specs=[hbm] * 10,
+            out_specs=[hbm] * 4,
+            scratch_shapes=[vm(*slab)] * 8
+            + [vm(rows + 8, ny, nz), vm(*slab), vm(*slab), vm(*slab), vm(*slab), vm(2, 8), vm(rows, ny // n_shot, nz)]
             + [
                 pltpu.VMEM((1, 1), jnp.int32),
                 vm(1, 2),
@@ -370,7 +384,6 @@
                 vm(8, traces),
                 vm(2, 8),
                 vm(8, 128),
-                vm(2, 8),
                 vm(5, 2, 4, ny, nz),
                 pltpu.VMEM((2 * nz, traces), BF16),
                 pltpu.VMEM((2 * traces, nz), BF16),
@@ -391,13 +404,21 @@
                 pltpu.SemaphoreType.DMA((count,)),
                 pltpu.SemaphoreType.DMA((count,)),
             ],
-            compiler_params=pltpu.CompilerParams(collective_id=0, has_side_effects=True, vmem_limit_bytes=40 << 20),
+            compiler_params=pltpu.CompilerParams(collective_id=0, has_side_effects=True, vmem_limit_bytes=56 << 20),
             cost_estimate=pl.CostEstimate(flops=10**9, bytes_accessed=2 << 20, transcendentals=0),
             name="two_steps",
         )(
             v, pm[0], p0[0], am[0], a0[0], cell.reshape(1, 1), wave,
             jnp.transpose(cells[0]), jnp.transpose(weights[0]), obs[0],
         )
+        f, a, r, g = pl.pallas_call(
+            store,
+            out_shape=results,
+            in_specs=[hbm] * 4,
+            out_specs=[hbm] * 4,
+            scratch_shapes=[vm(*r.shape) for r in results] + [pltpu.SemaphoreType.DMA((2, 4))],
+            name="store",
+        )(*out)
         return f[None], a[None], r[None], g
 
     field = P("shot", "space", None, None)

time: 74.7 us -> 65.3 us (0.87)
  the two profiles are of different devices: /device:TPU:64 before, /device:TPU:1 now
where the time goes in v2:
time: 65.3 us; the launch traced here: 65.1 us
  Pallas kernels  63.8 us (98%)
  between operations  1.29 us (2%)
    pallas_call x1, Pallas kernels, per_device(): pl.pallas_call(functools.partial(kernel, sizes), out_shape=results, in_sp...  62 us
    pallas_call x1, Pallas kernels, per_device(): pl.pallas_call(store, out_shape=results, in_specs=[hbm] * 4, out_specs=[h...  1.81 us

profile of v2, /device:TPU:1, one launch (start us, length us, event | category | flops | bytes accessed | tf_op | source)
XLA Modules:
  0.0 65.1 jit_solution(11756533409418431383)
XLA Ops:
  1.3 62.0 %two_steps.1 = (f32[8,64,128]{2,1,0:T(8,128)}, f32[8,64,128]{2,1,0:T(8,128)}, f32[2,8]{1,0:T(2,128)}, f32[8,8,128]{2,1,0:T(8,128)}) custom-call(f32[8,64,128]{2,1,0:T(8,128)} %v_in.1, f32[8,64,128]{2,1,0:T(8,128)} %bitcast.16, f32[8,64,128]{2,1,0:T(8,128)} %bitcast.17, f32[8,64,128]{2,1,0:T(8,128)} %bitcast.18, f32[8,64,128]{2,1,0:T(8,128)} %bitcast.19, ...), custom_call_target="tpu_custom_call" | custom-call | flops 1000000000 | bytes 2097152 | tf_op jit(solution)/shard_map/two_steps/pallas_call | solution.py:373
  63.2 1.8 %store.1 = (f32[8,64,128]{2,1,0:T(8,128)}, f32[8,64,128]{2,1,0:T(8,128)}, f32[2,8]{1,0:T(2,128)}, f32[8,8,128]{2,1,0:T(8,128)}) custom-call(f32[8,64,128]{2,1,0:T(8,128)} %get-tuple-element.12.refs_0_, f32[8,64,128]{2,1,0:T(8,128)} %get-tuple-element.13.refs_1_, f32[2,8]{1,0:T(2,128)} %get-tuple-element.14.refs_2_, f32[8,8,128]{2,1,0:T(8,128)} %get-tuple-element.15.refs_3_), custom_call_target="tpu_custom_call" | custom-call | tf_op jit(solution)/shard_map/store/pallas_call | solution.py:414

commit v3 on v2

--- a/solution.py
+++ b/solution.py
@@ -11,6 +11,9 @@
 F32, BF16 = jnp.float32, jnp.bfloat16
 coeffs = (-205.0 / 72.0, 8.0 / 5.0, -1.0 / 5.0, 8.0 / 315.0, -1.0 / 560.0)
 whole = (8064.0, -1008.0, 128.0, -9.0)
+
+
+CHUNKS = 1
 
 
 def split(f):
@@ -62,9 +65,9 @@
     sizes,
     v_in, pm_in, p0_in, am_in, a0_in, cell_in, wave_in, cells_in, weights_in, obs_in,
     f_out, a_out, r_out, g_out,
-    V, PM, P0, AM, A0, LAP0, P1, LAP1, A1, INJ0, terms, P2, A2, res, grad,
+    V, PM, P0, AM, A0, LAP0, P1, LAP1, A1, terms, P2, A2, res, grad,
     cell, wave, cells, weights, obs, obs_wide,
-    halo, ozT, oz, oyT, wx, dz, dy,
+    halo, outer, ozT, oz, oyT, wx, wv, vs, vs_in, dz, dy,
     part, part_in, arow, sums, sums_y, sums_z, sums_x, gin,
     load_sem, out_sem, send_sem, recv_sem,
 ):
@@ -144,6 +147,14 @@
     left_edge = jnp.where(s > 0, 1.0, 0.0).astype(F32)
     right_edge = jnp.where(s < n_space - 1, 1.0, 0.0).astype(F32)
 
+    def at_traces(f):
+        hi, lo = split(f)
+        g = dot(jnp.concatenate([hi.reshape(rows * ny, nz), lo.reshape(rows * ny, nz)], axis=1), ozT[...])
+        return [g[i * ny : (i + 1) * ny] for i in range(rows)]
+
+    def over_y(g):
+        return jnp.sum(g * oyT[...].astype(F32), axis=0, keepdims=True)
+
     for k in (2, 3, 4, 5, 6):
         loads[k].wait()
     place = cell[...] - s * (rows * ny * nz)
@@ -159,7 +170,10 @@
     a0 = A0[...]
     lap = lap_inside(a0, dz[...], dy[...])
     for i in range(rows):
-        A1[4 + i] = 2.0 * a0[i] - AM[i] + V[i] * lap[i]
+        A1[i] = 2.0 * a0[i] - AM[i] + V[i] * lap[i]
+
+    for i, g in enumerate(at_traces(V[...])):
+        vs[i // 4, pl.ds(i % 4, 1)] = over_y(g)
 
     loads[9].wait()
     lane0, row0 = (s * 8) % 128, (s * 8) // 128
@@ -171,60 +185,19 @@
 
     pl.semaphore_wait(barrier, len(partners))
 
-    def exchange(field, low, high):
-        a = send(low, halo.at[field, 1], ring(-1))
-        b = send(high, halo.at[field, 0], ring(1))
+    wide = ny // CHUNKS
+    parts = [pl.ds(c * wide, wide) for c in range(CHUNKS)]
+
+    def exchange(field, low, high, c):
+        a = send(low.at[:, parts[c]], halo.at[field, 1, :, parts[c]], ring(-1))
+        b = send(high.at[:, parts[c]], halo.at[field, 0, :, parts[c]], ring(1))
         return b, a
 
-    got_p0 = exchange(0, p0_in.at[lo4], p0_in.at[hi4])
-    got_a0 = exchange(1, a0_in.at[lo4], a0_in.at[hi4])
+    got_p0 = [exchange(0, p0_in.at[lo4], p0_in.at[hi4], c) for c in range(CHUNKS)]
     obs_y = [send(sums.at[0], sums_y.at[0, k], d) for k, d in enumerate(to_y)]
-    got_v = exchange(2, v_in.at[lo4], v_in.at[hi4])
-
-    got_p0[0].wait_recv()
-    hl = halo[0, 0]
-    for i in range(4):
-        add = from_left(hl, i, left_edge)
-        LAP0[i] += add
-        P1[i] += V[i] * add
-    p1_left = send(P1.at[lo4], halo.at[3, 1], ring(-1))
-    got_p0[1].wait_recv()
-    hr = halo[0, 1]
-    for i in range(4):
-        add = from_right(hr, i, right_edge)
-        LAP0[rows - 4 + i] += add
-        P1[rows - 4 + i] += V[rows - 4 + i] * add
-    p1_right = send(P1.at[hi4], halo.at[3, 0], ring(1))
-
-    def sample(f, k):
-        hi, lo = split(f)
-        g = dot(jnp.concatenate([hi.reshape(rows * ny, nz), lo.reshape(rows * ny, nz)], axis=1), ozT[...])
-        acc = wx[4:5] * g[0:ny]
-        for i in range(1, rows):
-            acc = acc + wx[4 + i : 5 + i] * g[i * ny : (i + 1) * ny]
-        line = jnp.sum(acc * oyT[...].astype(F32), axis=0, keepdims=True)
-        part[k] = jnp.zeros((8, 128), F32)
-        for b in range(blocks):
-            part[k, pl.ds(k * blocks + b, 1), :] = line[:, b * 128 : (b + 1) * 128]
-        return [send(part.at[k], part_in.at[k, i], d) for i, d in enumerate(near)]
-
-    p1 = P1[...]
-    got_part = [sample(p1, 0)]
-    lap = lap_inside(p1, dz[...], dy[...])
-    for i in range(rows):
-        LAP1[i] = lap[i]
-        P2[i] = 2.0 * p1[i] - P0[i] + V[i] * (lap[i] + spots[i] * wave[0:1, 1:2])
-
-    got_a0[0].wait_recv()
-    hl = halo[1, 0]
-    for i in range(4):
-        A1[4 + i] += V[i] * from_left(hl, i, left_edge)
-    b1_left = send(A1.at[pl.ds(4, 4)], halo.at[4, 1], ring(-1))
-    got_a0[1].wait_recv()
-    hr = halo[1, 1]
-    for i in range(4):
-        A1[rows + i] += V[rows - 4 + i] * from_right(hr, i, right_edge)
-    b1_right = send(A1.at[pl.ds(rows, 4)], halo.at[4, 0], ring(1))
+    got_a0 = [exchange(1, a0_in.at[lo4], a0_in.at[hi4], c) for c in range(CHUNKS)]
+    vs_right = send(vs.at[0], vs_in.at[1], ring(-1))
+    vs_left = send(vs.at[1], vs_in.at[0], ring(1))
 
     def gather(got, own, ref, slot, count):
         total = own
@@ -237,79 +210,138 @@
     sums[1] = gather(obs_y, sums[0], sums_y, 0, ny_ - 1)
     obs_z = [send(sums.at[1], sums_z.at[0, k], d) for k, d in enumerate(to_z)]
 
-    p1_right.wait_recv()
-    hl = halo[3, 0]
+    got_p1 = []
+    for c, ys in enumerate(parts):
+        got_p0[c][0].wait_recv()
+        hl = halo[0, 0, :, ys]
+        for i in range(4):
+            add = from_left(hl, i, left_edge)
+            LAP0[i, ys] += add
+            P1[i, ys] += V[i, ys] * add
+        got_p0[c][1].wait_recv()
+        hr = halo[0, 1, :, ys]
+        for i in range(4):
+            k = rows - 4 + i
+            add = from_right(hr, i, right_edge)
+            LAP0[k, ys] += add
+            P1[k, ys] += V[k, ys] * add
+        got_p1.append(exchange(2, P1.at[lo4], P1.at[hi4], c))
+
+    p1 = P1[...]
+    lines = [over_y(g) for g in at_traces(p1)]
+    lap = lap_inside(p1, dz[...], dy[...])
+    for i in range(rows):
+        LAP1[i] = lap[i]
+        P2[i] = 2.0 * p1[i] - P0[i] + V[i] * (lap[i] + spots[i] * wave[0:1, 1:2])
+    acc = functools.reduce(jnp.add, [wx[4 + i : 5 + i] * g for i, g in enumerate(at_traces(P2[...]))])
+    second = over_y(acc)
+    first = functools.reduce(jnp.add, [wx[4 + i : 5 + i] * lines[i] for i in range(rows)])
+    vs_left.wait_recv()
+    vs_right.wait_recv()
+    wv[pl.ds(0, 4)] = wx[0:4] * vs_in[0]
+    wv[pl.ds(4, 4)] = wx[4:8] * vs[0]
+    wv[pl.ds(8, 4)] = wx[8:12] * vs[1]
+    wv[pl.ds(12, 4)] = wx[12:16] * vs_in[1]
     for i in range(4):
-        add = from_left(hl, i, left_edge)
-        LAP1[i] += add
-        P2[i] += V[i] * add
-    p1_left.wait_recv()
-    hr = halo[3, 1]
-    for i in range(4):
-        add = from_right(hr, i, right_edge)
-        LAP1[rows - 4 + i] += add
-        P2[rows - 4 + i] += V[rows - 4 + i] * add
-    got_part.append(sample(P2[...], 1))
+        second = second + wv[i : i + 1] * from_right(lines[0:4], i, 1.0)
+        second = second + wv[rows + 4 + i : rows + 5 + i] * from_left(lines[rows - 4 :], i, 1.0)
+    for k, line in enumerate((first, second)):
+        for b in range(blocks):
+            part[pl.ds(k * blocks + b, 1), :] = line[:, b * 128 : (b + 1) * 128]
+    got_part = [send(part, part_in.at[i], d) for i, d in enumerate(near)]
+    res_y = [send(part, sums_y.at[1, k], d) for k, d in enumerate(to_y)]
+
+    got_b1 = []
+    for c, ys in enumerate(parts):
+        got_a0[c][0].wait_recv()
+        hl = halo[1, 0, :, ys]
+        for i in range(4):
+            A1[i, ys] += V[i, ys] * from_left(hl, i, left_edge)
+        got_a0[c][1].wait_recv()
+        hr = halo[1, 1, :, ys]
+        for i in range(4):
+            k = rows - 4 + i
+            A1[k, ys] += V[k, ys] * from_right(hr, i, right_edge)
+        got_b1.append(exchange(3, A1.at[lo4], A1.at[hi4], c))
+
+    sums[2] = gather(obs_z, sums[1], sums_z, 0, nz_ - 1)
+    obs_x = [send(sums.at[2], sums_x.at[0, k], d) for k, d in enumerate(to_x)]
+
+    for c, ys in enumerate(parts):
+        got_p1[c][0].wait_recv()
+        hl = halo[2, 0, :, ys]
+        for i in range(4):
+            add = from_left(hl, i, left_edge)
+            LAP1[i, ys] += add
+            P2[i, ys] += V[i, ys] * add
+        got_p1[c][1].wait_recv()
+        hr = halo[2, 1, :, ys]
+        for i in range(4):
+            k = rows - 4 + i
+            add = from_right(hr, i, right_edge)
+            LAP1[k, ys] += add
+            P2[k, ys] += V[k, ys] * add
     outs = [pltpu.make_async_copy(P2, f_out, out_sem.at[0])]
     outs[0].start()
-    sums[3] = part[0] + part[1]
-    res_y = [send(sums.at[3], sums_y.at[1, k], d) for k, d in enumerate(to_y)]
-
-    sums[2] = gather(obs_z, sums[1], sums_z, 0, nz_ - 1)
-    obs_x = [send(sums.at[2], sums_x.at[0, k], d) for k, d in enumerate(to_x)]
+
+    sums[4] = gather(res_y, part[...], sums_y, 1, ny_ - 1)
+    res_z = [send(sums.at[4], sums_z.at[1, k], d) for k, d in enumerate(to_z)]
+
+    observed = gather(obs_x, sums[2], sums_x, 0, nx_ - 1)
+    for c in got_part:
+        c.wait_recv()
+    arow[...] = functools.reduce(jnp.add, [part_in[i] for i in range(4)]) + part[...] - observed
 
     def inject(k, first, count):
-        arow[k] = gather(got_part[k], part[k], part_in, k, 4) - observed
-        line = jnp.concatenate([arow[k, pl.ds(k * blocks + b, 1), :] for b in range(blocks)], axis=1)
-        hi, lo = split(wx[pl.ds(first, count)] * line)
+        line = jnp.concatenate([arow[pl.ds(k * blocks + b, 1), :] for b in range(blocks)], axis=1)
+        hi, lo = split(wv[pl.ds(first, count)] * line)
         hot = oyT[...]
         lhs = jnp.concatenate(
             [jnp.concatenate([hot * hi[i : i + 1], hot * lo[i : i + 1]], axis=1) for i in range(count)], axis=0
         )
-        return dot(lhs, oz[...])
-
-    observed = gather(obs_x, sums[2], sums_x, 0, nx_ - 1)
-
-    inj = inject(0, 4, rows)
-    for i in range(rows):
-        INJ0[i] = V[i] * inj[i * ny : (i + 1) * ny]
-    got_v[0].wait_recv()
-    got_v[1].wait_recv()
-    b1_right.wait_recv()
-    b1_left.wait_recv()
-    b1_left.wait_send()
-    b1_right.wait_send()
-    sums[4] = gather(res_y, sums[3], sums_y, 1, ny_ - 1)
-    res_z = [send(sums.at[4], sums_z.at[1, k], d) for k, d in enumerate(to_z)]
+        inj = dot(lhs, oz[...])
+        return [inj[i * ny : (i + 1) * ny] for i in range(count)]
+
+    for pair in got_b1:
+        for c in pair:
+            c.wait_send()
     inj = inject(1, 0, rows + 8)
     for i in range(4):
-        A1[i] = halo[4, 0, i] * left_edge + halo[2, 0, i] * inj[i * ny : (i + 1) * ny]
-        k = rows + 4 + i
-        A1[k] = halo[4, 1, i] * right_edge + halo[2, 1, i] * inj[k * ny : (k + 1) * ny]
+        outer[0, i] = inj[i]
+        outer[1, i] = inj[rows + 4 + i]
     for i in range(rows):
-        k = 4 + i
-        A1[k] += V[i] * inj[k * ny : (k + 1) * ny]
+        A1[i] += inj[4 + i]
     a1 = A1[...]
-    lap = lap_inside(a1[4 : 4 + rows], dz[...], dy[...])
+    inj = inject(0, 4, rows)
+    lap = lap_inside(a1, dz[...], dy[...])
     scale = 1.0 / n_shot
     for i in range(rows):
-        lp = lap[i]
-        if i < 4:
-            lp = lp + from_left(a1[0:4], i, 1.0)
-        if i >= rows - 4:
-            lp = lp + from_right(a1[rows + 4 :], i - rows + 4, 1.0)
-        a2 = 2.0 * a1[4 + i] - A0[i] + V[i] * lp + INJ0[i]
+        a2 = 2.0 * a1[i] - A0[i] + V[i] * lap[i] + inj[i]
         A2[i] = a2
-        terms[i] = (a1[4 + i] * LAP1[i] + a2 * LAP0[i]) * scale
+        terms[i] = (a1[i] * LAP1[i] + a2 * LAP0[i]) * scale
+    for c, ys in enumerate(parts):
+        got_b1[c][0].wait_recv()
+        hl = halo[3, 0, :, ys] * left_edge + outer[0, :, ys]
+        for i in range(4):
+            add = V[i, ys] * from_left(hl, i, 1.0)
+            A2[i, ys] += add
+            terms[i, ys] += add * LAP0[i, ys] * scale
+        got_b1[c][1].wait_recv()
+        hr = halo[3, 1, :, ys] * right_edge + outer[1, :, ys]
+        for i in range(4):
+            k = rows - 4 + i
+            add = V[k, ys] * from_right(hr, i, 1.0)
+            A2[k, ys] += add
+            terms[k, ys] += add * LAP0[k, ys] * scale
     got_g = [
         send(terms.at[:, pl.ds(pl.multiple_of(d[0] * 8, 8), 8)], gin.at[k], d) for k, d in enumerate(to_shot)
     ]
+    outs.append(pltpu.make_async_copy(A2, a_out, out_sem.at[1]))
+    outs[1].start()
 
     sums[5] = gather(res_z, sums[4], sums_z, 1, nz_ - 1)
     res_x = [send(sums.at[5], sums_x.at[1, k], d) for k, d in enumerate(to_x)]
 
-    outs.append(pltpu.make_async_copy(A2, a_out, out_sem.at[1]))
-    outs[1].start()
     total = terms[:, pl.ds(pl.multiple_of(h * 8, 8), 8)]
     for c in got_g:
         c.wait_recv()
@@ -333,8 +365,9 @@
     outs.append(pltpu.make_async_copy(res, r_out, out_sem.at[3]))
     outs[3].start()
 
+    done = [c for pair in got_b1 for c in pair]
     for c in sent:
-        if c is not b1_left and c is not b1_right:
+        if not any(c is d for d in done):
             c.wait_send()
     for c in outs:
         c.wait()
@@ -363,7 +396,7 @@
         slab = (rows, ny, nz)
         hbm = pl.BlockSpec(memory_space=pltpu.HBM)
         vm = lambda *shape: pltpu.VMEM(shape, F32)
-        count = 5 * 2 + 2 * 4 + 2 * (sizes[2] + sizes[3] + sizes[4] - 3) + n_shot - 1
+        count = 8 * CHUNKS + 2 + 4 + 2 * (sizes[2] + sizes[3] + sizes[4] - 3) + n_shot - 1
         results = (
                 jax.ShapeDtypeStruct(slab, F32),
                 jax.ShapeDtypeStruct(slab, F32),
@@ -375,8 +408,8 @@
             out_shape=results,
             in_specs=[hbm] * 10,
             out_specs=[hbm] * 4,
-            scratch_shapes=[vm(*slab)] * 8
-            + [vm(rows + 8, ny, nz), vm(*slab), vm(*slab), vm(*slab), vm(*slab), vm(2, 8), vm(rows, ny // n_shot, nz)]
+            scratch_shapes=[vm(*slab)] * 12
+            + [vm(2, 8), vm(rows, ny // n_shot, nz)]
             + [
                 pltpu.VMEM((1, 1), jnp.int32),
                 vm(1, 2),
@@ -384,16 +417,20 @@
                 vm(8, traces),
                 vm(2, 8),
                 vm(8, 128),
-                vm(5, 2, 4, ny, nz),
+                vm(4, 2, 4, ny, nz),
+                vm(2, 4, ny, nz),
                 pltpu.VMEM((2 * nz, traces), BF16),
                 pltpu.VMEM((2 * traces, nz), BF16),
                 pltpu.VMEM((ny, traces), BF16),
                 vm(rows + 8, traces),
+                vm(rows + 8, traces),
+                vm(2, 4, traces),
+                vm(2, 4, traces),
                 pltpu.VMEM((2 * nz, nz), BF16),
                 pltpu.VMEM((ny, 2 * ny), BF16),
-                vm(2, 8, 128),
-                vm(2, 4, 8, 128),
-                vm(2, 8, 128),
+                vm(8, 128),
+                vm(4, 8, 128),
+                vm(8, 128),
                 vm(6, 8, 128),
                 vm(2, sizes[4] - 1, 8, 128),
                 vm(2, sizes[3] - 1, 8, 128),

time: 65.3 us -> 55.3 us (0.85)
  Pallas kernels: 63.8 us -> 53.8 us
    pallas_call x1, Pallas kernels: 62 us -> 52 us  [per_device(): pl.pallas_call(functools.partial(kernel, sizes), out_shape=results, in_sp...]
where the time goes in v3:
time: 55.3 us; the launch traced here: 55.1 us
  Pallas kernels  53.8 us (97%)
  between operations  1.29 us (2%)
    pallas_call x1, Pallas kernels, per_device(): pl.pallas_call(functools.partial(kernel, sizes), out_shape=results, in_sp...  52 us
    pallas_call x1, Pallas kernels, per_device(): pl.pallas_call(store, out_shape=results, in_specs=[hbm] * 4, out_specs=[h...  1.81 us

profile of v3, /device:TPU:1, one launch (start us, length us, event | category | flops | bytes accessed | tf_op | source)
XLA Modules:
  0.0 55.1 jit_solution(14796228871070162971)
XLA Ops:
  1.3 52.0 %two_steps.1 = (f32[8,64,128]{2,1,0:T(8,128)}, f32[8,64,128]{2,1,0:T(8,128)}, f32[2,8]{1,0:T(2,128)}, f32[8,8,128]{2,1,0:T(8,128)}) custom-call(f32[8,64,128]{2,1,0:T(8,128)} %v_in.1, f32[8,64,128]{2,1,0:T(8,128)} %bitcast.16, f32[8,64,128]{2,1,0:T(8,128)} %bitcast.17, f32[8,64,128]{2,1,0:T(8,128)} %bitcast.18, f32[8,64,128]{2,1,0:T(8,128)} %bitcast.19, ...), custom_call_target="tpu_custom_call" | custom-call | flops 1000000000 | bytes 2097152 | tf_op jit(solution)/shard_map/two_steps/pallas_call | solution.py:406
  53.3 1.8 %store.1 = (f32[8,64,128]{2,1,0:T(8,128)}, f32[8,64,128]{2,1,0:T(8,128)}, f32[2,8]{1,0:T(2,128)}, f32[8,8,128]{2,1,0:T(8,128)}) custom-call(f32[8,64,128]{2,1,0:T(8,128)} %get-tuple-element.12.refs_0_, f32[8,64,128]{2,1,0:T(8,128)} %get-tuple-element.13.refs_1_, f32[2,8]{1,0:T(2,128)} %get-tuple-element.14.refs_2_, f32[8,8,128]{2,1,0:T(8,128)} %get-tuple-element.15.refs_3_), custom_call_target="tpu_custom_call" | custom-call | tf_op jit(solution)/shard_map/store/pallas_call | solution.py:451

commit v4 on v3

--- a/solution.py
+++ b/solution.py
@@ -64,12 +64,12 @@
 def kernel(
     sizes,
     v_in, pm_in, p0_in, am_in, a0_in, cell_in, wave_in, cells_in, weights_in, obs_in,
-    f_out, a_out, r_out, g_out,
-    V, PM, P0, AM, A0, LAP0, P1, LAP1, A1, terms, P2, A2, res, grad,
+    P2, A2, res, grad,
+    V, PM, P0, AM, A0, LAP0, P1, LAP1, A1, terms,
     cell, wave, cells, weights, obs, obs_wide,
     halo, outer, ozT, oz, oyT, wx, wv, vs, vs_in, dz, dy,
     part, part_in, arow, sums, sums_y, sums_z, sums_x, gin,
-    load_sem, out_sem, send_sem, recv_sem,
+    load_sem, send_sem, recv_sem,
 ):
     n_shot, n_space, nx_, nz_, ny_ = sizes
     rows, ny, nz = V.shape
@@ -193,9 +193,9 @@
         b = send(high.at[:, parts[c]], halo.at[field, 0, :, parts[c]], ring(1))
         return b, a
 
-    got_p0 = [exchange(0, p0_in.at[lo4], p0_in.at[hi4], c) for c in range(CHUNKS)]
+    got_p0 = [exchange(0, P0.at[lo4], P0.at[hi4], c) for c in range(CHUNKS)]
     obs_y = [send(sums.at[0], sums_y.at[0, k], d) for k, d in enumerate(to_y)]
-    got_a0 = [exchange(1, a0_in.at[lo4], a0_in.at[hi4], c) for c in range(CHUNKS)]
+    got_a0 = [exchange(1, A0.at[lo4], A0.at[hi4], c) for c in range(CHUNKS)]
     vs_right = send(vs.at[0], vs_in.at[1], ring(-1))
     vs_left = send(vs.at[1], vs_in.at[0], ring(1))
 
@@ -281,8 +281,6 @@
             add = from_right(hr, i, right_edge)
             LAP1[k, ys] += add
             P2[k, ys] += V[k, ys] * add
-    outs = [pltpu.make_async_copy(P2, f_out, out_sem.at[0])]
-    outs[0].start()
 
     sums[4] = gather(res_y, part[...], sums_y, 1, ny_ - 1)
     res_z = [send(sums.at[4], sums_z.at[1, k], d) for k, d in enumerate(to_z)]
@@ -319,25 +317,35 @@
         a2 = 2.0 * a1[i] - A0[i] + V[i] * lap[i] + inj[i]
         A2[i] = a2
         terms[i] = (a1[i] * LAP1[i] + a2 * LAP0[i]) * scale
-    for c, ys in enumerate(parts):
-        got_b1[c][0].wait_recv()
-        hl = halo[3, 0, :, ys] * left_edge + outer[0, :, ys]
-        for i in range(4):
-            add = V[i, ys] * from_left(hl, i, 1.0)
-            A2[i, ys] += add
-            terms[i, ys] += add * LAP0[i, ys] * scale
-        got_b1[c][1].wait_recv()
-        hr = halo[3, 1, :, ys] * right_edge + outer[1, :, ys]
-        for i in range(4):
-            k = rows - 4 + i
-            add = V[k, ys] * from_right(hr, i, 1.0)
-            A2[k, ys] += add
-            terms[k, ys] += add * LAP0[k, ys] * scale
-    got_g = [
-        send(terms.at[:, pl.ds(pl.multiple_of(d[0] * 8, 8), 8)], gin.at[k], d) for k, d in enumerate(to_shot)
-    ]
-    outs.append(pltpu.make_async_copy(A2, a_out, out_sem.at[1]))
-    outs[1].start()
+    def finish_left():
+        for c, ys in enumerate(parts):
+            got_b1[c][0].wait_recv()
+            hl = halo[3, 0, :, ys] * left_edge + outer[0, :, ys]
+            for i in range(4):
+                add = V[i, ys] * from_left(hl, i, 1.0)
+                A2[i, ys] += add
+                terms[i, ys] += add * LAP0[i, ys] * scale
+
+    def finish_right():
+        for c, ys in enumerate(parts):
+            got_b1[c][1].wait_recv()
+            hr = halo[3, 1, :, ys] * right_edge + outer[1, :, ys]
+            for i in range(4):
+                k = rows - 4 + i
+                add = V[k, ys] * from_right(hr, i, 1.0)
+                A2[k, ys] += add
+                terms[k, ys] += add * LAP0[k, ys] * scale
+
+    got_g = []
+    for stage in range(2):
+        right_now = (x == 0) if stage == 0 else (x != 0)
+        pl.when(right_now)(finish_right)
+        pl.when(jnp.logical_not(right_now))(finish_left)
+        half = pl.ds(jnp.where(right_now, rows - 4, 0), 4)
+        got_g += [
+            send(terms.at[half, pl.ds(pl.multiple_of(d[0] * 8, 8), 8)], gin.at[k, half], d)
+            for k, d in enumerate(to_shot)
+        ]
 
     sums[5] = gather(res_z, sums[4], sums_z, 1, nz_ - 1)
     res_x = [send(sums.at[5], sums_x.at[1, k], d) for k, d in enumerate(to_x)]
@@ -348,8 +356,6 @@
     for k in range(n_shot - 1):
         total = total + gin[k]
     grad[...] = total
-    outs.append(pltpu.make_async_copy(grad, g_out, out_sem.at[2]))
-    outs[2].start()
 
     every = gather(res_x, sums[5], sums_x, 1, nx_ - 1)
     picked = jnp.concatenate(
@@ -362,27 +368,18 @@
     obs_wide[pl.ds(0, 2)] = picked
     rolled = pltpu.roll(obs_wide[...], (128 - lane0) % 128, 1)
     res[...] = rolled[0:2, 0:8] - obs[...]
-    outs.append(pltpu.make_async_copy(res, r_out, out_sem.at[3]))
-    outs[3].start()
 
     done = [c for pair in got_b1 for c in pair]
     for c in sent:
         if not any(c is d for d in done):
             c.wait_send()
-    for c in outs:
-        c.wait()
 
 
 def store(*refs):
-    given, given_back, held, sems = refs[:4], refs[4:8], refs[8:12], refs[12]
-    loads = [pltpu.make_async_copy(a, b, sems.at[0, i]) for i, (a, b) in enumerate(zip(given, held))]
-    stores = [pltpu.make_async_copy(a, b, sems.at[1, i]) for i, (a, b) in enumerate(zip(held, given_back))]
-    for c in loads:
+    copies = [pltpu.make_async_copy(a, b, refs[8].at[i]) for i, (a, b) in enumerate(zip(refs[:4], refs[4:8]))]
+    for c in copies:
         c.start()
-    for c, d in zip(loads, stores):
-        c.wait()
-        d.start()
-    for c in stores:
+    for c in copies:
         c.wait()
 
 
@@ -395,8 +392,9 @@
         traces = weights.shape[1]
         slab = (rows, ny, nz)
         hbm = pl.BlockSpec(memory_space=pltpu.HBM)
+        vmem = pl.BlockSpec(memory_space=pltpu.VMEM)
         vm = lambda *shape: pltpu.VMEM(shape, F32)
-        count = 8 * CHUNKS + 2 + 4 + 2 * (sizes[2] + sizes[3] + sizes[4] - 3) + n_shot - 1
+        count = 8 * CHUNKS + 2 + 4 + 2 * (sizes[2] + sizes[3] + sizes[4] - 3) + 2 * (n_shot - 1)
         results = (
                 jax.ShapeDtypeStruct(slab, F32),
                 jax.ShapeDtypeStruct(slab, F32),
@@ -405,11 +403,10 @@
             )
         out = pl.pallas_call(
             functools.partial(kernel, sizes),
-            out_shape=results,
+            out_shape=tuple(pltpu.VMEM(r.shape, F32) for r in results),
             in_specs=[hbm] * 10,
-            out_specs=[hbm] * 4,
-            scratch_shapes=[vm(*slab)] * 12
-            + [vm(2, 8), vm(rows, ny // n_shot, nz)]
+            out_specs=[vmem] * 4,
+            scratch_shapes=[vm(*slab)] * 10
             + [
                 pltpu.VMEM((1, 1), jnp.int32),
                 vm(1, 2),
@@ -437,25 +434,29 @@
                 vm(2, sizes[2] - 1, 8, 128),
                 vm(n_shot - 1, rows, ny // n_shot, nz),
                 pltpu.SemaphoreType.DMA((10,)),
-                pltpu.SemaphoreType.DMA((4,)),
                 pltpu.SemaphoreType.DMA((count,)),
                 pltpu.SemaphoreType.DMA((count,)),
             ],
-            compiler_params=pltpu.CompilerParams(collective_id=0, has_side_effects=True, vmem_limit_bytes=56 << 20),
+            compiler_params=pltpu.CompilerParams(collective_id=0, has_side_effects=True, vmem_limit_bytes=40 << 20),
             cost_estimate=pl.CostEstimate(flops=10**9, bytes_accessed=2 << 20, transcendentals=0),
             name="two_steps",
         )(
-            v, pm[0], p0[0], am[0], a0[0], cell.reshape(1, 1), wave,
-            jnp.transpose(cells[0]), jnp.transpose(weights[0]), obs[0],
+            *(
+                o if o.size == 1 else pltpu.with_memory_space_constraint(o, pltpu.HBM)
+                for o in (
+                    v, pm[0], p0[0], am[0], a0[0], cell.reshape(1, 1), wave,
+                    jnp.transpose(cells[0]), jnp.transpose(weights[0]), obs[0],
+                )
+            )
         )
         f, a, r, g = pl.pallas_call(
             store,
             out_shape=results,
-            in_specs=[hbm] * 4,
+            in_specs=[vmem] * 4,
             out_specs=[hbm] * 4,
-            scratch_shapes=[vm(*r.shape) for r in results] + [pltpu.SemaphoreType.DMA((2, 4))],
+            scratch_shapes=[pltpu.SemaphoreType.DMA((4,))],
             name="store",
-        )(*out)
+        )(*(pltpu.with_memory_space_constraint(o, pltpu.VMEM) for o in out))
         return f[None], a[None], r[None], g
 
     field = P("shot", "space", None, None)

time: 55.3 us -> 52.6 us (0.951)
  Pallas kernels: 53.8 us -> 51.2 us
    pallas_call x2, Pallas kernels: 53.8 us -> 51.2 us  [the longest x1 50.3 us: per_device(): pl.pallas_call(functools.partial(kernel, sizes), out_shape=tuple((pltpu.V...]
where the time goes in v4:
time: 52.6 us; the launch traced here: 52.5 us
  Pallas kernels  51.2 us (97%)
  between operations  1.29 us (2%)
    pallas_call x1, Pallas kernels, per_device(): pl.pallas_call(functools.partial(kernel, sizes), out_shape=tuple((pltpu.V...  50.3 us

profile of v4, /device:TPU:1, one launch (start us, length us, event | category | flops | bytes accessed | tf_op | source)
XLA Modules:
  0.0 52.5 jit_solution(17802628812988389960)
XLA Ops:
  1.3 50.3 %two_steps.1 = (f32[8,64,128]{2,1,0:T(8,128)S(1)}, f32[8,64,128]{2,1,0:T(8,128)S(1)}, f32[2,8]{1,0:T(2,128)S(1)}, f32[8,8,128]{2,1,0:T(8,128)S(1)}) custom-call(f32[8,64,128]{2,1,0:T(8,128)} %v_in.1, f32[8,64,128]{2,1,0:T(8,128)} %bitcast.16, f32[8,64,128]{2,1,0:T(8,128)} %bitcast.17, f32[8,64,128]{2,1,0:T(8,128)} %bitcast.18, f32[8,64,128]{2,1,0:T(8,128)} %bitcast.19, ...), custom_call_target="tpu_custom_call" | custom-call | flops 1000000000 | bytes 2097152 | tf_op jit(solution)/shard_map/two_steps/pallas_call | solution.py:404
  51.6 0.8 %store.1 = (f32[8,64,128]{2,1,0:T(8,128)}, f32[8,64,128]{2,1,0:T(8,128)}, f32[2,8]{1,0:T(2,128)}, f32[8,8,128]{2,1,0:T(8,128)}) custom-call(f32[8,64,128]{2,1,0:T(8,128)S(1)} %get-tuple-element.12.refs_0_, f32[8,64,128]{2,1,0:T(8,128)S(1)} %get-tuple-element.13.refs_1_, f32[2,8]{1,0:T(2,128)S(1)} %get-tuple-element.14.refs_2_, ...), custom_call_target="tpu_custom_call" | custom-call | tf_op jit(solution)/shard_map/store/pallas_call | solution.py:452

commit v5 on v4

--- a/solution.py
+++ b/solution.py
@@ -59,6 +59,17 @@
 
 def from_right(h, i, edge):
     return functools.reduce(jnp.add, [(coeffs[j] * edge) * h[i + j - 4] for j in range(4 - i, 5)])
+
+
+class Halo:
+    def __init__(self, copy, sends, receives):
+        self.copy, self.sends, self.receives = copy, sends, receives
+
+    def wait_send(self):
+        pl.when(self.sends)(self.copy.wait_send)
+
+    def wait_recv(self):
+        pl.when(self.receives)(self.copy.wait_recv)
 
 
 def kernel(
@@ -92,7 +103,11 @@
     near = [ring(1), ring(-1), ring(2), ring(-2)]
 
     barrier = pltpu.get_barrier_semaphore()
-    partners = near + to_z + to_y + to_x + to_shot
+    has = [s < n_space - 1, s > 0, s < n_space - 2, s > 1]
+    comes = [has[1], has[0], has[3], has[2]]
+    for d, there in zip(near, has):
+        pl.when(there)(lambda d=d: pl.semaphore_signal(barrier, inc=1, device_id=d, device_id_type=MESH))
+    partners = to_z + to_y + to_x + to_shot
     for d in partners:
         pl.semaphore_signal(barrier, inc=1, device_id=d, device_id_type=MESH)
 
@@ -144,6 +159,20 @@
         acc = acc + jnp.where(at_x[k : k + 1] == row_id, w[k : k + 1], 0.0)
     wx[...] = acc
 
+    for side, end in ((0, s == 0), (1, s == n_space - 1)):
+
+        @pl.when(end)
+        def _(side=side):
+            for field in range(4):
+                halo[field, side] = jnp.zeros((4, ny, nz), F32)
+            vs_in[side] = jnp.zeros((4, traces), F32)
+
+    for i in range(4):
+
+        @pl.when(jnp.logical_not(comes[i]))
+        def _(i=i):
+            part_in[i] = jnp.zeros((8, 128), F32)
+
     left_edge = jnp.where(s > 0, 1.0, 0.0).astype(F32)
     right_edge = jnp.where(s < n_space - 1, 1.0, 0.0).astype(F32)
 
@@ -183,21 +212,30 @@
     which = iota((8, 128), 0)
     sums[0] = jnp.where(which == row0, rolled[0:1], 0.0) + jnp.where(which == blocks + row0, rolled[1:2], 0.0)
 
-    pl.semaphore_wait(barrier, len(partners))
+    pl.semaphore_wait(barrier, len(partners) + sum(jnp.where(there, 1, 0) for there in has))
 
     wide = ny // CHUNKS
     parts = [pl.ds(c * wide, wide) for c in range(CHUNKS)]
 
+    def between(src, dst, to, sends, receives):
+        i = len(sent)
+        copy = pltpu.make_async_remote_copy(
+            src_ref=src, dst_ref=dst, send_sem=send_sem.at[i], recv_sem=recv_sem.at[i], device_id=to, device_id_type=MESH
+        )
+        sent.append(Halo(copy, sends, receives))
+        pl.when(sends)(copy.start)
+        return sent[-1]
+
     def exchange(field, low, high, c):
-        a = send(low.at[:, parts[c]], halo.at[field, 1, :, parts[c]], ring(-1))
-        b = send(high.at[:, parts[c]], halo.at[field, 0, :, parts[c]], ring(1))
+        a = between(low.at[:, parts[c]], halo.at[field, 1, :, parts[c]], ring(-1), s > 0, s < n_space - 1)
+        b = between(high.at[:, parts[c]], halo.at[field, 0, :, parts[c]], ring(1), s < n_space - 1, s > 0)
         return b, a
 
     got_p0 = [exchange(0, P0.at[lo4], P0.at[hi4], c) for c in range(CHUNKS)]
     obs_y = [send(sums.at[0], sums_y.at[0, k], d) for k, d in enumerate(to_y)]
     got_a0 = [exchange(1, A0.at[lo4], A0.at[hi4], c) for c in range(CHUNKS)]
-    vs_right = send(vs.at[0], vs_in.at[1], ring(-1))
-    vs_left = send(vs.at[1], vs_in.at[0], ring(1))
+    vs_right = between(vs.at[0], vs_in.at[1], ring(-1), has[1], has[0])
+    vs_left = between(vs.at[1], vs_in.at[0], ring(1), has[0], has[1])
 
     def gather(got, own, ref, slot, count):
         total = own
@@ -248,7 +286,7 @@
     for k, line in enumerate((first, second)):
         for b in range(blocks):
             part[pl.ds(k * blocks + b, 1), :] = line[:, b * 128 : (b + 1) * 128]
-    got_part = [send(part, part_in.at[i], d) for i, d in enumerate(near)]
+    got_part = [between(part, part_in.at[i], d, has[i], comes[i]) for i, d in enumerate(near)]
     res_y = [send(part, sums_y.at[1, k], d) for k, d in enumerate(to_y)]
 
     got_b1 = []

time: 52.6 us -> 52.6 us (level)
  the two profiles are of different devices: /device:TPU:1 before, /device:TPU:7 now
where the time goes in v5:
time: 52.6 us; the launch traced here: 52.4 us
  Pallas kernels  51.1 us (97%)
  between operations  1.29 us (2%)
    pallas_call x1, Pallas kernels, per_device(): pl.pallas_call(functools.partial(kernel, sizes), out_shape=tuple((pltpu.V...  50.3 us

profile of v5, /device:TPU:7, one launch (start us, length us, event | category | flops | bytes accessed | tf_op | source)
XLA Modules:
  0.0 52.4 jit_solution(11548584548516737511)
XLA Ops:
  1.3 50.3 %two_steps.1 = (f32[8,64,128]{2,1,0:T(8,128)S(1)}, f32[8,64,128]{2,1,0:T(8,128)S(1)}, f32[2,8]{1,0:T(2,128)S(1)}, f32[8,8,128]{2,1,0:T(8,128)S(1)}) custom-call(f32[8,64,128]{2,1,0:T(8,128)} %v_in.1, f32[8,64,128]{2,1,0:T(8,128)} %bitcast.16, f32[8,64,128]{2,1,0:T(8,128)} %bitcast.17, f32[8,64,128]{2,1,0:T(8,128)} %bitcast.18, f32[8,64,128]{2,1,0:T(8,128)} %bitcast.19, ...), custom_call_target="tpu_custom_call" | custom-call | flops 1000000000 | bytes 2097152 | tf_op jit(solution)/shard_map/two_steps/pallas_call | solution.py:442
  51.6 0.8 %store.1 = (f32[8,64,128]{2,1,0:T(8,128)}, f32[8,64,128]{2,1,0:T(8,128)}, f32[2,8]{1,0:T(2,128)}, f32[8,8,128]{2,1,0:T(8,128)}) custom-call(f32[8,64,128]{2,1,0:T(8,128)S(1)} %get-tuple-element.12.refs_0_, f32[8,64,128]{2,1,0:T(8,128)S(1)} %get-tuple-element.13.refs_1_, f32[2,8]{1,0:T(2,128)S(1)} %get-tuple-element.14.refs_2_, ...), custom_call_target="tpu_custom_call" | custom-call | tf_op jit(solution)/shard_map/store/pallas_call | solution.py:490
